TPU v7x, 768 devices: a whole 4x8x12 slice. The times are simulated.
768 devices in a mesh: row: 24 (over z_hi, y), col: 32 (over x, z_lo, core).
Axes of the slice: x: 4, y: 8, z: 12 (z_hi: 3, z_lo: 4; z = z_hi * 4 + z_lo), core: 2. Of those that a mesh axis runs over, the one named last changes fastest.
Arguments:
- activations: bfloat16 [3072, 28672], P('row', 'col'), may hold values from -6 to 6
- gradients: bfloat16 [3072, 6144], P('col', 'row'), may hold values from -0.29882812 to 0.29882812
- seq_example: int32 [6], replicated, may hold values from 0 to 2, as said below
Outputs:
- eigen_corr: float32 [6144, 28672], P('row', 'col')
Inputs may be any that keep to these rules, and one draw needn't show every extreme that they name: `seq_example`: every one of the 3 examples owns at least one of the 6 sequences.
All inputs are finite; a program needn't handle non-finite values.
Results may differ from a plain program's by a relative error of at most 0.0003.
Values may be sent and summed in bfloat16 or wider, within the bound.
A program may use at most 32 MiB of HBM per device.

v0:
```python
import jax
import jax.numpy as jnp
from jax import lax
from jax.sharding import PartitionSpec as P

SEQLEN = 512
SEQS = 6
EXAMPLES = 3


def on_device(activations, gradients, seq_example):
    grads_all = lax.all_gather(gradients, "col", axis=0, tiled=True)
    out_tile = grads_all.shape[1]
    in_tile = activations.shape[1]
    acts_all = lax.all_gather(activations, "row", axis=0, tiled=True)
    seq_grad = jnp.einsum(
        "sto,stc->soc",
        grads_all.reshape(SEQS, SEQLEN, out_tile),
        acts_all.reshape(SEQS, SEQLEN, in_tile),
        preferred_element_type=jnp.float32,
    )
    member = (seq_example[None, :] == jnp.arange(EXAMPLES, dtype=jnp.int32)[:, None]).astype(
        jnp.float32
    )
    example_grad = jnp.einsum("ns,soc->noc", member, seq_grad, precision=lax.Precision.HIGHEST)
    return jnp.sum(example_grad * example_grad, axis=0) / EXAMPLES


def solution(mesh):
    placed = (P("row", "col"), P("col", "row"), P())
    return jax.shard_map(
        on_device, mesh=mesh, in_specs=placed, out_specs=P("row", "col"), check_vma=False
    )
```

profile of v0, /device:TPU:2, one launch (start us, length us, event | category | flops | bytes accessed | tf_op | source)
XLA Modules:
  0.0 279.7 jit_solution(3082255841370902851)
XLA Ops:
  6.5 0.0 all-gather.3.cloned.1.call-start
  6.5 0.7 all-gather.3.cloned.1.call-update
  7.3 0.0 all-gather.5.cloned.1.call-start
  7.3 0.7 all-gather.5.cloned.1.call-update
  8.0 73.8 %all-gather.3.cloned.1.call-done = bf16[3072,256]{1,0:T(8,128)(2,1)} async-done(((bf16[96,256]{1,0:T(8,128)(2,1)}), bf16[3072,256]{1,0:T(8,128)(2,1)}) %all-gather.3.cloned.1.call-update) | async-done | bytes 1572880 | tf_op jit(solution)/shard_map/all_gather | solution.py:12
  81.8 176.4 %all-gather.5.cloned.1.call-done = bf16[3072,896]{1,0:T(8,128)(2,1)} async-done(((bf16[128,896]{1,0:T(8,128)(2,1)}), bf16[3072,896]{1,0:T(8,128)(2,1)}) %all-gather.5.cloned.1.call-update) | async-done | bytes 5505040 | tf_op jit(solution)/shard_map/all_gather | solution.py:15
  258.2 0.0 copy-start
  258.2 4.9 %fusion.7 = f32[6,256,896]{2,1,0:T(8,128)S(1)} fusion(bf16[6,512,256]{2,1,0:T(8,128)(2,1)} %bitcast.8, bf16[6,512,896]{2,1,0:T(8,128)(2,1)} %bitcast.7), kind=kOutput, calls=%fused_computation.7 | convolution fusion | flops 1409286144 | bytes 12582912 | tf_op jit(solution)/shard_map/sto,stc->soc/dot_general | solution.py:16
  263.1 0.0 copy-done
  263.1 8.8 %multiply_reduce_fusion = f32[256,896]{1,0:T(8,128)S(1)} fusion(f32[6,256,896]{2,1,0:T(8,128)S(1)} %fusion.7, s32[6]{0:T(128)S(1)} %copy-done), kind=kOutput, calls=%fused_computation.2 | convolution fusion | flops 50692112 | bytes 6422552 | tf_op jit(solution)/shard_map/ns,soc->noc/dot_general | solution.py:25
  271.9 1.0 broadcast_multiply_fusion
Async XLA Ops:
  6.5 75.2 %all-gather.3.cloned.1.call-start = ((), (), s32[]{:S(2)}) async-start(), calls=%async_computation | async-start | bytes 1622016 | tf_op jit(solution)/shard_map/all_gather | solution.py:12
  7.3 250.9 %all-gather.5.cloned.1.call-start = ((), (), s32[]{:S(2)}) async-start(), calls=%async_computation.1 | async-start | bytes 5734400 | tf_op jit(solution)/shard_map/all_gather | solution.py:15
  258.2 4.9 %copy-start = (s32[6]{0:T(128)S(1)}, s32[6]{0:T(128)}, u32[]{:S(2)}) copy-start(s32[6]{0:T(128)} %param.5) | copy-start | bytes 76
Sparse Core Ops, SparseCore 0:
  9.8 71.9 all-gather.2
  85.8 172.3 all-gather.4
where the time goes:
time: 280 us
  waiting for transfers between devices  252 us (90%)
  matrix products  13.7 us (5%)
  between operations  13.4 us (5%)
    all_gather x1, waiting for transfers between devices, on_device(): acts_all = lax.all_gather(activations, 'row', axis=0, tiled=True)  176 us
    all_gather x1, waiting for transfers between devices, on_device(): grads_all = lax.all_gather(gradients, 'col', axis=0, tiled=True)  73.8 us
    dot_general x1, matrix products, on_device(): jnp.einsum('ns,soc->noc', member, seq_grad, precision=lax.Precision.HIGHEST)  8.76 us
  transfers between devices with their start and end apart: 2, of which 2 were waited for; matrix products, arithmetic and copies ran while one was open for 0% of the time, Pallas kernels for 0%

commit v1 on v0

v1 whole, which is shorter than its diff:
```python
import jax
import jax.numpy as jnp
from jax import lax
from jax.experimental import pallas as pl
from jax.experimental.pallas import tpu as pltpu
from jax.sharding import PartitionSpec as P

MESH = pl.DeviceIdType.MESH
SEQLEN = 512
SEQS = 6
EXAMPLES = 3
TOKENS = 3072
NX, NY, NZH, NZL = 4, 8, 3, 4
BLK = TOKENS // (NY * NZH)
GBLK = TOKENS // (NX * NZL * 2)
WIDE = 256
NWIDE = 3
LAST = 128
HALF = BLK // 2
OUT_TILE = 256
IN_TILE = 896
UNITS = [(0, 0), (0, 1), (0, 2), (1, 0), (2, 0), (1, 1), (2, 1), (1, 2), (2, 2)]
START = {0: 0, 1: 0, 2: 0, 3: 3, 4: 3, 5: 4, 6: 4, 7: 5, 8: 5}


def body(seq_ref, acts_ref, grads_ref, out_ref, abuf, gmine, gall, obuf,
         loc_sem, out_sem, az_s, az_r, ay_s, ay_r, bz_s, bz_r, by_s, by_r, g1_s, g1_r, g2_s, g2_r, g3_s, g3_r):
    row, col = lax.axis_index("row"), lax.axis_index("col")
    zh, y = row // NY, row % NY
    x, zl, core = col // (2 * NZL), (col // 2) % NZL, col % 2

    def at_y(d):
        return (zh * NY + (y + d + NY) % NY, col)

    def at_z(d):
        return (((zh + d) % NZH) * NY + y, col)

    def at_zl(d):
        return (row, x * (2 * NZL) + ((zl + d) % NZL) * 2 + core)

    def at_x(d):
        return (row, ((x + d) % NX) * (2 * NZL) + zl * 2 + core)

    other = (row, col + 1 - 2 * core)
    peers = [at_y(1), at_y(-1), at_z(1), at_z(2)] + [at_zl(d) for d in (1, 2, 3)] + [at_x(d) for d in (1, 2, 3)] + [other]

    def tok(dz, dy, half=None):
        start = (((zh + dz) % NZH) * NY + (y + dy + NY) % NY) * BLK
        if half is None:
            return pl.ds(pl.multiple_of(start, BLK), BLK)
        return pl.ds(pl.multiple_of(start + half * HALF, HALF), HALF)

    def cols(j):
        return pl.ds(j * WIDE, WIDE if j < NWIDE else LAST)

    def copy(ref, src, ssem, rsem, to):
        return pltpu.make_async_remote_copy(
            src_ref=ref.at[src], dst_ref=ref.at[src], send_sem=ssem, recv_sem=rsem, device_id=to, device_id_type=MESH
        )

    sent = []

    def send(*args):
        c = copy(*args)
        c.start()
        sent.append(c)

    own_a = pltpu.make_async_copy(acts_ref, abuf.at[tok(0, 0), :], loc_sem.at[0])
    own_a.start()
    gslot = (x * NZL + zl) * GBLK

    def gtok(x_of, zl_of, n=1):
        return pl.ds(pl.multiple_of((x_of * NZL + zl_of) * GBLK, GBLK), n * GBLK)

    own_g = pltpu.make_async_copy(grads_ref, gmine.at[gtok(x, zl), :], loc_sem.at[1])
    own_g.start()
    barrier = pltpu.get_barrier_semaphore()
    for peer in peers:
        pl.semaphore_signal(barrier, inc=1, device_id=peer, device_id_type=MESH)
    pl.semaphore_wait(barrier, len(peers))
    own_g.wait()
    own_a.wait()

    def ring(ref, c, dz, h, way, ssem, rsem, go):
        step = 1 if way == 0 else -1
        half = None if h < 4 else way
        if go:
            send(ref, (tok(dz, -step * (h - 1), half), c), ssem, rsem, at_y(step))
        else:
            copy(ref, (tok(dz, -step * h, half), c), ssem, rsem, at_y(step)).wait_recv()

    def a_hop(u, h, go):
        dz, j = UNITS[u]
        for way in (0, 1):
            k = (u * 4 + h - 1) * 2 + way
            ring(abuf, cols(j), dz, h, way, ay_s.at[k], ay_r.at[k], go)

    def b_hop(h, go):
        for way in (0, 1):
            k = (h - 1) * 2 + way
            ring(abuf, cols(NWIDE), 0, h, way, by_s.at[k], by_r.at[k], go)

    def a_z_wait(u):
        dz, j = UNITS[u]
        k = j * 2 + dz - 1
        copy(abuf, (tok(dz, 0), cols(j)), az_s.at[k], az_r.at[k], at_z(dz)).wait_recv()

    def a_z_send(j):
        for d in (1, 2):
            k = j * 2 + (NZH - d) - 1
            send(abuf, (tok(0, 0), cols(j)), az_s.at[k], az_r.at[k], at_z(d))

    def b_z(dy, go):
        for d in (1, 2):
            dz = NZH - d
            k = (dy + 3) * 2 + dz - 1
            if go:
                send(abuf, (tok(0, dy), cols(NWIDE)), bz_s.at[k], bz_r.at[k], at_z(d))
            else:
                copy(abuf, (tok(dz, dy), cols(NWIDE)), bz_s.at[k], bz_r.at[k], at_z(d)).wait_recv()

    def g1(d, go):
        if go:
            send(gmine, (gtok(x, zl), slice(None)), g1_s.at[d - 1], g1_r.at[d - 1], at_zl(d))
        else:
            src = (gtok(x, (zl - d + NZL) % NZL), slice(None))
            copy(gmine, src, g1_s.at[d - 1], g1_r.at[d - 1], at_zl(d)).wait_recv()

    def g2(d, go):
        if go:
            send(gmine, (gtok(x, 0, NZL), slice(None)), g2_s.at[d - 1], g2_r.at[d - 1], at_x(d))
        else:
            src = (gtok((x - d + NX) % NX, 0, NZL), slice(None))
            copy(gmine, src, g2_s.at[d - 1], g2_r.at[d - 1], at_x(d)).wait_recv()

    gother = gall.at[1, pl.ds(0, TOKENS // 2), :]
    g3 = pltpu.make_async_remote_copy(
        src_ref=gmine, dst_ref=gother, send_sem=g3_s, recv_sem=g3_r, device_id=other, device_id_type=MESH
    )

    member = [[jnp.where(seq_ref[s] == n, 1.0, 0.0).astype(jnp.float32) for s in range(SEQS)] for n in range(EXAMPLES)]
    outs = []

    def compute(j):
        c = cols(j)
        totals = [None] * EXAMPLES
        for s in range(SEQS):
            part = lax.dot_general(
                gfull[s * SEQLEN:(s + 1) * SEQLEN, :],
                abuf[s * SEQLEN:(s + 1) * SEQLEN, c],
                (((0,), (0,)), ((), ())),
                preferred_element_type=jnp.float32,
            )
            for n in range(EXAMPLES):
                term = member[n][s] * part
                totals[n] = term if s == 0 else totals[n] + term
        total = sum(t * t for t in totals)
        obuf[:, c] = total / EXAMPLES
        out = pltpu.make_async_copy(obuf.at[:, c], out_ref.at[:, c], out_sem.at[j])
        out.start()
        outs.append(out)

    gfull = gall.at[0]
    last_wave = max(START.values()) + 4
    for w in range(last_wave):
        for u in range(len(UNITS)):
            h = w - START[u] + 1
            if h < 1 or h > 4:
                continue
            if h == 1 and UNITS[u][0] != 0:
                a_z_wait(u)
            if h > 1:
                a_hop(u, h - 1, False)
            a_hop(u, h, True)
        if w == 0:
            for d in (1, 2, 3):
                g1(d, True)
            for j in range(NWIDE):
                a_z_send(j)
            b_hop(1, True)
        if w == 1:
            for d in (1, 2, 3):
                g1(d, False)
            for d in (1, 2, 3):
                g2(d, True)
        if w in (1, 2, 3):
            b_hop(w, False)
            b_hop(w + 1, True)
        if w == 3:
            for d in (1, 2, 3):
                g2(d, False)
            g3.start()
        if w == 4:
            b_hop(4, False)
            b_z(0, True)
            b_z(1, True)
            b_z(-1, True)
        if w == 5:
            for dy in (2, -2, 3):
                b_z(dy, True)
            g3.wait_recv()
            for b in range(NX * NZL):
                mine = gmine[b * GBLK:(b + 1) * GBLK, :]
                theirs = gother[b * GBLK:(b + 1) * GBLK, :]
                first = jnp.where(core == 0, mine, theirs)
                second = jnp.where(core == 0, theirs, mine)
                gfull[2 * b * GBLK:(2 * b + 1) * GBLK, :] = first
                gfull[(2 * b + 1) * GBLK:(2 * b + 2) * GBLK, :] = second
        if w == 6:
            for dy in (-3, 4):
                b_z(dy, True)
        for j in range(NWIDE - 1):
            if w == START[UNITS.index((2, j))] + 4:
                for u, (dz, jj) in enumerate(UNITS):
                    if jj == j:
                        a_hop(u, 4, False)
                compute(j)
    for dy in (0, 1, -1, 2, -2, 3, -3, 4):
        b_z(dy, False)
    compute(NWIDE)
    for u, (dz, jj) in enumerate(UNITS):
        if jj == NWIDE - 1:
            a_hop(u, 4, False)
    compute(NWIDE - 1)
    for c in sent:
        c.wait_send()
    g3.wait_send()
    for out in outs:
        out.wait()


def on_device(activations, gradients, seq_example):
    dma = pltpu.SemaphoreType.DMA
    nu = len(UNITS)
    return pl.pallas_call(
        body,
        out_shape=jax.ShapeDtypeStruct((OUT_TILE, IN_TILE), jnp.float32),
        in_specs=[
            pl.BlockSpec(memory_space=pltpu.SMEM),
            pl.BlockSpec(memory_space=pl.ANY),
            pl.BlockSpec(memory_space=pl.ANY),
        ],
        out_specs=pl.BlockSpec(memory_space=pl.ANY),
        scratch_shapes=[
            pltpu.VMEM((TOKENS, IN_TILE), jnp.bfloat16),
            pltpu.VMEM((TOKENS // 2, OUT_TILE), jnp.bfloat16),
            pltpu.VMEM((2, TOKENS, OUT_TILE), jnp.bfloat16),
            pltpu.VMEM((OUT_TILE, IN_TILE), jnp.float32),
            dma((2,)),
            dma((NWIDE + 1,)),
            dma((2 * NWIDE,)),
            dma((2 * NWIDE,)),
            dma((nu * 8,)),
            dma((nu * 8,)),
            dma((16,)),
            dma((16,)),
            dma((8,)),
            dma((8,)),
            dma((3,)),
            dma((3,)),
            dma((3,)),
            dma((3,)),
            dma,
            dma,
        ],
        compiler_params=pltpu.CompilerParams(collective_id=0, has_side_effects=True, vmem_limit_bytes=40 << 20),
        cost_estimate=pl.CostEstimate(
            flops=2 * TOKENS * OUT_TILE * IN_TILE, bytes_accessed=OUT_TILE * IN_TILE * 4, transcendentals=0
        ),
        name="gather_and_correct",
    )(seq_example, activations, gradients)


def solution(mesh):
    placed = (P("row", "col"), P("col", "row"), P())
    return jax.shard_map(
        on_device, mesh=mesh, in_specs=placed, out_specs=P("row", "col"), check_vma=False
    )
```

time: 280 us -> 81.9 us (0.29)
  the two profiles are of different devices: /device:TPU:2 before, /device:TPU:64 now
where the time goes in v1:
time: 81.9 us; the launch traced here: 81.7 us
  Pallas kernels  78.4 us (96%)
  local copies, waits for them, and re-layouts  3.32 us (4%)
    pallas_call x1, Pallas kernels, on_device(): pl.pallas_call(body, out_shape=jax.ShapeDtypeStruct((OUT_TILE, IN_TILE),...  78.4 us
    unnamed x7, local copies, waits for them, and re-layouts  3.32 us

profile of v1, /device:TPU:64, one launch (start us, length us, event | category | flops | bytes accessed | tf_op | source)
XLA Modules:
  0.0 81.7 jit_solution(10453682178685112940)
XLA Ops:
  0.0 0.0 copy-start
  0.0 0.9 %copy-done = bf16[128,896]{1,0:T(8,128)(2,1)S(1)} copy-done((bf16[128,896]{1,0:T(8,128)(2,1)S(1)}, bf16[128,896]{1,0:T(8,128)(2,1)}, u32[]{:S(2)}) %copy-start) | copy-done | bytes 229400
  0.9 0.0 copy-start.1
  0.9 0.8 copy-done.1
  1.7 0.0 copy-start.2
  1.7 0.7 copy-done.2
  2.4 78.4 %gather_and_correct.1 = f32[256,896]{1,0:T(8,128)S(1)} custom-call(s32[6]{0:T(128)S(1)} %copy-done.2, bf16[128,896]{1,0:T(8,128)(2,1)S(1)} %copy-done, bf16[96,256]{1,0:T(8,128)(2,1)S(1)} %copy-done.1), custom_call_target="tpu_custom_call" | custom-call | flops 1409286144 | bytes 917504 | tf_op jit(solution)/shard_map/gather_and_correct/pallas_call | solution.py:235
  80.8 0.9 %copy.5 = f32[256,896]{1,0:T(8,128)} copy(f32[256,896]{1,0:T(8,128)S(1)} %gather_and_correct.1) | data formatting | bytes 1835008
Async XLA Ops:
  0.0 0.9 %copy-start = (bf16[128,896]{1,0:T(8,128)(2,1)S(1)}, bf16[128,896]{1,0:T(8,128)(2,1)}, u32[]{:S(2)}) copy-start(bf16[128,896]{1,0:T(8,128)(2,1)} %acts_ref.1) | copy-start | bytes 688132
  0.9 0.8 copy-start.1
  1.7 0.7 copy-start.2

commit v2 on v0

v2 whole, which is shorter than its diff:
```python
import jax
import jax.numpy as jnp
from jax import lax
from jax.experimental import pallas as pl
from jax.experimental.pallas import tpu as pltpu
from jax.sharding import PartitionSpec as P

MESH = pl.DeviceIdType.MESH
SEQLEN = 512
SEQS = 6
EXAMPLES = 3
TOKENS = 3072
NX, NY, NZH, NZL = 4, 8, 3, 4
BLK = TOKENS // (NY * NZH)
GBLK = TOKENS // (NX * NZL * 2)
NR = 2
PART = BLK // NR
OUT_TILE = 256
IN_TILE = 896
FIRST = (768,) * NR
UNITS = [(b, r) for b in range(NZH) for r in range(NR)]
CHUNKS = [(0, 256), (256, 256), (512, 256), (768, 128)]
START = {(b, r): 0.01 * r if b == 0 else 1.6 + 1.5 * b + 0.5 * r for b, r in UNITS}
Z_DOWN = [0.2 + 0.01 * r for r in range(NR)]
Z_LATE = [1.1, 2.05]
LATE = [0, 3]
Z_UP = [1.5 + 0.01 * r for r in range(NR)]
G1_DOWN, G1_UP, G2_WHEN, G3_WHEN, ORDER_WHEN = 0.15, 1.05, 4.6, 6.05, 7.5
SPREAD = [(4.4, (0, 1, -1)), (5.4, (2, -2, 3)), (6.4, (-3, 4))]
OWN_WHEN = 7.65
SECOND_WHEN = 8.2


def body(seq_ref, acts_ref, grads_ref, out_ref, abuf, gmine, gother, gfull, sums, obuf,
         loc_sem, out_sem, az_s, az_r, ay_s, ay_r, bz_s, bz_r, g1_s, g1_r, g2_s, g2_r, g3_s, g3_r, hi_sem, lo_sem, x_sem, core_sem):
    row, col = lax.axis_index("row"), lax.axis_index("col")
    zh, y = row // NY, row % NY
    x, zl, core = col // (2 * NZL), (col // 2) % NZL, col % 2
    planes = [zh, jnp.where(zh == 0, 1, 0), jnp.where(zh == 2, 1, 2)]

    def at_y(d):
        return (zh * NY + (y + d + NY) % NY, col)

    def at_z(b):
        return (planes[b] * NY + y, col)

    def at_zl(d):
        return (row, x * (2 * NZL) + ((zl + d) % NZL) * 2 + core)

    def at_x(d):
        return (row, ((x + d) % NX) * (2 * NZL) + zl * 2 + core)

    other = (row, col + 1 - 2 * core)

    def tok(b, dy, r=None):
        start = (planes[b] * NY + (y + dy + NY) % NY) * BLK
        if r is None:
            return pl.ds(pl.multiple_of(start, BLK), BLK)
        return pl.ds(pl.multiple_of(start + r * PART, PART), PART)

    def gtok(x_of, zl_of, n=1):
        return pl.ds(pl.multiple_of((x_of * NZL + zl_of) * GBLK, GBLK), n * GBLK)

    own_a = pltpu.make_async_copy(acts_ref, abuf.at[tok(0, 0), :], loc_sem.at[0])
    own_a.start()
    own_g = pltpu.make_async_copy(grads_ref, gmine.at[gtok(x, zl), :], loc_sem.at[1])
    own_g.start()

    corner = (x == 0) & (y == 0) & (core == 0)

    def rank(z):
        return jnp.where(corner & (z == 0), NZH * NZL, z)

    mine = rank(zh * NZL + zl)
    later_z = [None] + [rank(planes[b] * NZL + zl) > mine for b in (1, 2)]
    later_zl = [None] + [rank(zh * NZL + (zl + d) % NZL) > mine for d in (1, 2, 3)]
    later_x = [None] + [(x + d) % NX < x for d in (1, 2, 3)]
    pairs = [(later_z[b], at_z(b), hi_sem.at[zh]) for b in (1, 2)]
    pairs += [(later_zl[d], at_zl(d), lo_sem.at[zl]) for d in (1, 2, 3)]
    pairs += [(later_x[d], at_x(d), x_sem.at[x]) for d in (1, 2, 3)]
    pairs += [(core == 1, other, core_sem)]

    barrier = pltpu.get_barrier_semaphore()
    for peer in (at_y(1), at_y(-1)):
        pl.semaphore_signal(barrier, inc=1, device_id=peer, device_id_type=MESH)
    before_me = 2
    for later, peer, _ in pairs:
        before_me += jnp.where(later, 0, 1)

        @pl.when(later)
        def _():
            pl.semaphore_signal(barrier, inc=1, device_id=peer, device_id_type=MESH)
    pl.semaphore_wait(barrier, before_me)
    for later, peer, sem in pairs:
        @pl.when(jnp.logical_not(later))
        def _():
            pl.semaphore_signal(sem, inc=1, device_id=peer, device_id_type=MESH)
    own_a.wait()
    own_g.wait()

    def copy(ref, src, ssem, rsem, to):
        return pltpu.make_async_remote_copy(
            src_ref=ref.at[src], dst_ref=ref.at[src], send_sem=ssem, recv_sem=rsem, device_id=to, device_id_type=MESH
        )

    sent = []

    def send(*args):
        c = copy(*args)
        c.start()
        sent.append(c)

    def width(u):
        b, r = UNITS[u]
        return slice(None) if b == 0 else pl.ds(0, FIRST[r])

    def hop(u, way, h, go):
        b, r = UNITS[u]
        step = 1 if way == 0 else -1
        k = (u * 2 + way) * 4 + h - 1
        at = tok(b, -step * (h - 1 if go else h), r), width(u)
        if go:
            send(abuf, at, ay_s.at[k], ay_r.at[k], at_y(step))
        else:
            copy(abuf, at, ay_s.at[k], ay_r.at[k], at_y(step)).wait_recv()

    def last_hop(u, way):
        b, r = UNITS[u]
        return 4 if (r + b) % 2 == way else 3

    def y_step(u, h):
        b, r = UNITS[u]
        if h == 1 and b > 0:
            z_copy(r, b, b).wait_recv()
        for way in (0, 1):
            if 1 < h <= last_hop(u, way) + 1:
                hop(u, way, h - 1, False)
            if h <= last_hop(u, way):
                hop(u, way, h, True)

    def their(b):
        return jnp.where(zh > 3 - zh - planes[b], 2, 1)

    def z_copy(r, plane, number):
        k = (number - 1) * NR + r
        return copy(abuf, (tok(plane, 0, r), pl.ds(0, FIRST[r])), az_s.at[k], az_r.at[k], at_z(max(plane, 1)))

    def z_out(r, b):
        return pltpu.make_async_remote_copy(
            src_ref=abuf.at[tok(0, 0, r), pl.ds(0, FIRST[r])],
            dst_ref=abuf.at[tok(0, 0, r), pl.ds(0, FIRST[r])],
            send_sem=az_s.at[(b - 1) * NR + r],
            recv_sem=az_r.at[(their(b) - 1) * NR + r],
            device_id=at_z(b),
            device_id_type=MESH,
        )

    def z_up(r):
        for b in (1, 2):
            @pl.when(later_z[b])
            def _():
                if r == 0:
                    pl.semaphore_wait(hi_sem.at[planes[b]], 1)
                z_out(r, b).start()

    def z_down(r, first):
        for b in (1, 2):
            late = (planes[b] == (zh + 2) % NZH) & (zl < LATE[r])

            @pl.when(jnp.logical_not(later_z[b]) & (jnp.logical_not(late) if first else late))
            def _():
                z_out(r, b).start()

    def rest(dy, go):
        for b in (1, 2):
            for r in range(NR):
                if FIRST[r] == IN_TILE:
                    continue
                c = pl.ds(FIRST[r], IN_TILE - FIRST[r])
                k = (dy + 3) * 2 * NR + r
                if go:
                    send(abuf, (tok(0, dy, r), c), bz_s.at[k + NR * (b - 1)], bz_r.at[k + NR * (their(b) - 1)], at_z(b))
                else:
                    copy(abuf, (tok(b, dy, r), c), bz_s.at[k + NR * (b - 1)], bz_r.at[k + NR * (b - 1)], at_z(b)).wait_recv()

    def spread(*dys):
        for dy in dys:
            rest(dy, True)

    def g1_copy(d):
        return copy(gmine, (gtok(x, zl), slice(None)), g1_s.at[d - 1], g1_r.at[d - 1], at_zl(d))

    def g1_send(up):
        for d in (1, 2, 3):
            there = (zl + d) % NZL

            @pl.when(later_zl[d] if up else jnp.logical_not(later_zl[d]))
            def _():
                if up:
                    pl.semaphore_wait(lo_sem.at[there], 1)
                g1_copy(d).start()

    def g2_send():
        for d in (1, 2, 3):
            src = (gtok(x, (zl - d + NZL) % NZL), slice(None))
            copy(gmine, src, g1_s.at[d - 1], g1_r.at[d - 1], at_zl(d)).wait_recv()
        for d in (1, 2, 3):
            @pl.when(later_x[d])
            def _():
                pl.semaphore_wait(x_sem.at[(x + d) % NX], 1)
            send(gmine, (gtok(x, 0, NZL), slice(None)), g2_s.at[d - 1], g2_r.at[d - 1], at_x(d))

    g3 = pltpu.make_async_remote_copy(
        src_ref=gmine, dst_ref=gother, send_sem=g3_s, recv_sem=g3_r, device_id=other, device_id_type=MESH
    )

    def g3_send():
        for d in (1, 2, 3):
            src = (gtok((x - d + NX) % NX, 0, NZL), slice(None))
            copy(gmine, src, g2_s.at[d - 1], g2_r.at[d - 1], at_x(d)).wait_recv()

        @pl.when(core == 1)
        def _():
            pl.semaphore_wait(core_sem, 1)
        g3.start()

    def g_order():
        g3.wait_recv()
        for k in range(NX * NZL):
            ours = gmine[k * GBLK:(k + 1) * GBLK, :]
            theirs = gother[k * GBLK:(k + 1) * GBLK, :]
            gfull[2 * k * GBLK:(2 * k + 1) * GBLK, :] = jnp.where(core == 0, ours, theirs)
            gfull[(2 * k + 1) * GBLK:(2 * k + 2) * GBLK, :] = jnp.where(core == 0, theirs, ours)

    def seq_grad(b, i, c):
        at = pl.ds(pl.multiple_of((planes[b] * 2 + i) * SEQLEN, SEQLEN), SEQLEN)
        return lax.dot_general(
            gfull[at, :], abuf[at, c], (((0,), (0,)), ((), ())), preferred_element_type=jnp.float32
        )

    member = [
        [[jnp.where(seq_ref[planes[b] * 2 + i] == n, 1.0, 0.0) for i in (0, 1)] for b in range(NZH)]
        for n in range(EXAMPLES)
    ]

    def added(b, e, before, pair):
        for i in (0, 1):
            term = member[e][b][i] * pair[i]
            before = term if before is None else before + term
        return before

    def fold(b, chunks):
        for c0, n in chunks:
            c = pl.ds(c0, n)
            pair = [seq_grad(b, i, c) for i in (0, 1)]
            for e in range(EXAMPLES):
                sums[e, :, c] = added(b, e, None if b == 0 else sums[e, :, c], pair)

    events = [(START[UNITS[u]] + h - 1, y_step, u, h) for u in range(len(UNITS)) for h in (1, 2, 3, 4, 5)]
    events += [(when, z_down, r, True) for r, when in enumerate(Z_DOWN)]
    events += [(when, z_down, r, False) for r, when in enumerate(Z_LATE)]
    events += [(when, z_up, r) for r, when in enumerate(Z_UP)]
    events += [(when, spread, *dys) for when, dys in SPREAD]
    events += [(G1_DOWN, g1_send, False), (G1_UP, g1_send, True)]
    events += [(G2_WHEN, g2_send), (G3_WHEN, g3_send), (ORDER_WHEN, g_order), (OWN_WHEN, fold, 0, CHUNKS)]
    events += [(SECOND_WHEN, fold, 1, [c for c in CHUNKS if c[0] < min(FIRST)])]
    for _, what, *given in sorted(events, key=lambda e: e[0]):
        what(*given)
    for dy in range(-3, 5):
        rest(dy, False)

    outs = []
    for k, (c0, n) in enumerate(CHUNKS):
        c = pl.ds(c0, n)
        if c0 >= min(FIRST):
            fold(1, [(c0, n)])
        pair = [seq_grad(2, i, c) for i in (0, 1)]
        totals = [added(2, e, sums[e, :, c], pair) for e in range(EXAMPLES)]
        obuf[:, c] = sum(t * t for t in totals) / EXAMPLES
        out = pltpu.make_async_copy(obuf.at[:, c], out_ref.at[:, c], out_sem.at[k])
        out.start()
        outs.append(out)

    for b in (1, 2):
        for r in range(NR):
            z_out(r, b).wait_send()
    for d in (1, 2, 3):
        g1_copy(d).wait_send()
    for c in sent:
        c.wait_send()
    g3.wait_send()
    for out in outs:
        out.wait()


def on_device(activations, gradients, seq_example):
    dma, vmem = pltpu.SemaphoreType.DMA, pltpu.VMEM
    return pl.pallas_call(
        body,
        out_shape=jax.ShapeDtypeStruct((OUT_TILE, IN_TILE), jnp.float32),
        in_specs=[
            pl.BlockSpec(memory_space=pltpu.SMEM),
            pl.BlockSpec(memory_space=pl.ANY),
            pl.BlockSpec(memory_space=pl.ANY),
        ],
        out_specs=pl.BlockSpec(memory_space=pl.ANY),
        scratch_shapes=[
            vmem((TOKENS, IN_TILE), jnp.bfloat16),
            vmem((TOKENS // 2, OUT_TILE), jnp.bfloat16),
            vmem((TOKENS // 2, OUT_TILE), jnp.bfloat16),
            vmem((TOKENS, OUT_TILE), jnp.bfloat16),
            vmem((EXAMPLES, OUT_TILE, IN_TILE), jnp.float32),
            vmem((OUT_TILE, IN_TILE), jnp.float32),
            dma((2,)),
            dma((len(CHUNKS),)),
            dma((2 * NR,)),
            dma((2 * NR,)),
            dma((len(UNITS) * 8,)),
            dma((len(UNITS) * 8,)),
            dma((16 * NR,)),
            dma((16 * NR,)),
            dma((3,)),
            dma((3,)),
            dma((3,)),
            dma((3,)),
            dma,
            dma,
            pltpu.SemaphoreType.REGULAR((NZH,)),
            pltpu.SemaphoreType.REGULAR((NZL,)),
            pltpu.SemaphoreType.REGULAR((NX,)),
            pltpu.SemaphoreType.REGULAR,
        ],
        compiler_params=pltpu.CompilerParams(collective_id=0, has_side_effects=True, vmem_limit_bytes=58 << 20),
        cost_estimate=pl.CostEstimate(
            flops=2 * TOKENS * OUT_TILE * IN_TILE, bytes_accessed=OUT_TILE * IN_TILE * 4, transcendentals=0
        ),
        name="gather_and_correct",
    )(seq_example, activations, gradients)


def solution(mesh):
    placed = (P("row", "col"), P("col", "row"), P())
    return jax.shard_map(
        on_device, mesh=mesh, in_specs=placed, out_specs=P("row", "col"), check_vma=False
    )
```

time: 280 us -> 75.7 us (0.27)
  the two profiles are of different devices: /device:TPU:2 before, /device:TPU:72 now
where the time goes in v2:
time: 75.7 us; the launch traced here: 75.5 us
  Pallas kernels  73.3 us (97%)
  local copies, waits for them, and re-layouts  2.16 us (3%)
    pallas_call x1, Pallas kernels, on_device(): pl.pallas_call(body, out_shape=jax.ShapeDtypeStruct((OUT_TILE, IN_TILE),...  73.3 us
    unnamed x1, local copies, waits for them, and re-layouts  2.16 us

profile of v2, /device:TPU:72, one launch (start us, length us, event | category | flops | bytes accessed | tf_op | source)
XLA Modules:
  0.0 75.5 jit_solution(15137418527845590073)
XLA Ops:
  0.0 73.3 %gather_and_correct.1 = f32[256,896]{1,0:T(8,128)} custom-call(s32[6]{0:T(128)} %seq_ref.1, bf16[128,896]{1,0:T(8,128)(2,1)} %acts_ref.1, bf16[96,256]{1,0:T(8,128)(2,1)} %grads_ref.1), custom_call_target="tpu_custom_call" | custom-call | flops 1409286144 | bytes 917504 | tf_op jit(solution)/shard_map/gather_and_correct/pallas_call | solution.py:298
  73.3 2.2 %copy.5 = f32[256,896]{1,0:T(8,128)} copy(f32[256,896]{1,0:T(8,128)} %gather_and_correct.1) | data formatting | bytes 1835008

commit v3 on v2

--- a/solution.py
+++ b/solution.py
@@ -17,21 +17,23 @@
 PART = BLK // NR
 OUT_TILE = 256
 IN_TILE = 896
-FIRST = (768,) * NR
+FIRST = 768
+NREST = 2
+REST_PART = NY * BLK // NREST
 UNITS = [(b, r) for b in range(NZH) for r in range(NR)]
 CHUNKS = [(0, 256), (256, 256), (512, 256), (768, 128)]
-START = {(b, r): 0.01 * r if b == 0 else 1.6 + 1.5 * b + 0.5 * r for b, r in UNITS}
+START = {(b, r): 0.01 * r if b == 0 else 1.6 + 1.5 * b + 0.9 * r for b, r in UNITS}
 Z_DOWN = [0.2 + 0.01 * r for r in range(NR)]
 Z_LATE = [1.1, 2.05]
 LATE = [0, 3]
 Z_UP = [1.5 + 0.01 * r for r in range(NR)]
 G1_DOWN, G1_UP, G2_WHEN, G3_WHEN, ORDER_WHEN = 0.15, 1.05, 4.6, 6.05, 7.5
-SPREAD = [(4.4, (0, 1, -1)), (5.4, (2, -2, 3)), (6.4, (-3, 4))]
+SPREAD = 4.15
 OWN_WHEN = 7.65
 SECOND_WHEN = 8.2
 
 
-def body(seq_ref, acts_ref, grads_ref, out_ref, abuf, gmine, gother, gfull, sums, obuf,
+def body(seq_ref, acts_ref, grads_ref, out_ref, abuf, gmine, gother, gfull, sums, rest_own, rest_far, obuf,
          loc_sem, out_sem, az_s, az_r, ay_s, ay_r, bz_s, bz_r, g1_s, g1_r, g2_s, g2_r, g3_s, g3_r, hi_sem, lo_sem, x_sem, core_sem):
     row, col = lax.axis_index("row"), lax.axis_index("col")
     zh, y = row // NY, row % NY
@@ -112,7 +114,7 @@
 
     def width(u):
         b, r = UNITS[u]
-        return slice(None) if b == 0 else pl.ds(0, FIRST[r])
+        return slice(None) if b == 0 else pl.ds(0, FIRST)
 
     def hop(u, way, h, go):
         b, r = UNITS[u]
@@ -143,12 +145,12 @@
 
     def z_copy(r, plane, number):
         k = (number - 1) * NR + r
-        return copy(abuf, (tok(plane, 0, r), pl.ds(0, FIRST[r])), az_s.at[k], az_r.at[k], at_z(max(plane, 1)))
+        return copy(abuf, (tok(plane, 0, r), pl.ds(0, FIRST)), az_s.at[k], az_r.at[k], at_z(max(plane, 1)))
 
     def z_out(r, b):
         return pltpu.make_async_remote_copy(
-            src_ref=abuf.at[tok(0, 0, r), pl.ds(0, FIRST[r])],
-            dst_ref=abuf.at[tok(0, 0, r), pl.ds(0, FIRST[r])],
+            src_ref=abuf.at[tok(0, 0, r), pl.ds(0, FIRST)],
+            dst_ref=abuf.at[tok(0, 0, r), pl.ds(0, FIRST)],
             send_sem=az_s.at[(b - 1) * NR + r],
             recv_sem=az_r.at[(their(b) - 1) * NR + r],
             device_id=at_z(b),
@@ -171,21 +173,33 @@
             def _():
                 z_out(r, b).start()
 
-    def rest(dy, go):
-        for b in (1, 2):
-            for r in range(NR):
-                if FIRST[r] == IN_TILE:
-                    continue
-                c = pl.ds(FIRST[r], IN_TILE - FIRST[r])
-                k = (dy + 3) * 2 * NR + r
-                if go:
-                    send(abuf, (tok(0, dy, r), c), bz_s.at[k + NR * (b - 1)], bz_r.at[k + NR * (their(b) - 1)], at_z(b))
-                else:
-                    copy(abuf, (tok(b, dy, r), c), bz_s.at[k + NR * (b - 1)], bz_r.at[k + NR * (b - 1)], at_z(b)).wait_recv()
-
-    def spread(*dys):
-        for dy in dys:
-            rest(dy, True)
+    def rest(b, p):
+        at = pl.ds(p * REST_PART, REST_PART)
+        return pltpu.make_async_remote_copy(
+            src_ref=rest_own.at[at],
+            dst_ref=rest_far.at[their(b) - 1, at],
+            send_sem=bz_s.at[(b - 1) * NREST + p],
+            recv_sem=bz_r.at[(their(b) - 1) * NREST + p],
+            device_id=at_z(b),
+            device_id_type=MESH,
+        )
+
+    def spread():
+        rest_own[...] = abuf[pl.ds(pl.multiple_of(zh * (NY * BLK), NY * BLK), NY * BLK), FIRST:IN_TILE]
+        for p in range(NREST):
+            for b in (1, 2):
+                rest(b, p).start()
+
+    def rest_wait(b, p):
+        at = pl.ds(p * REST_PART, REST_PART)
+        pltpu.make_async_remote_copy(
+            src_ref=rest_own.at[at],
+            dst_ref=rest_far.at[b - 1, at],
+            send_sem=bz_s.at[(b - 1) * NREST + p],
+            recv_sem=bz_r.at[(b - 1) * NREST + p],
+            device_id=at_z(b),
+            device_id_type=MESH,
+        ).wait_recv()
 
     def g1_copy(d):
         return copy(gmine, (gtok(x, zl), slice(None)), g1_s.at[d - 1], g1_r.at[d - 1], at_zl(d))
@@ -234,8 +248,12 @@
 
     def seq_grad(b, i, c):
         at = pl.ds(pl.multiple_of((planes[b] * 2 + i) * SEQLEN, SEQLEN), SEQLEN)
+        if b > 0 and c.start >= FIRST:
+            acts = rest_far[b - 1, i * SEQLEN:(i + 1) * SEQLEN, c.start - FIRST:c.start - FIRST + c.size]
+        else:
+            acts = abuf[at, c]
         return lax.dot_general(
-            gfull[at, :], abuf[at, c], (((0,), (0,)), ((), ())), preferred_element_type=jnp.float32
+            gfull[at, :], acts, (((0,), (0,)), ((), ())), preferred_element_type=jnp.float32
         )
 
     member = [
@@ -260,19 +278,20 @@
     events += [(when, z_down, r, True) for r, when in enumerate(Z_DOWN)]
     events += [(when, z_down, r, False) for r, when in enumerate(Z_LATE)]
     events += [(when, z_up, r) for r, when in enumerate(Z_UP)]
-    events += [(when, spread, *dys) for when, dys in SPREAD]
+    events += [(SPREAD, spread)]
     events += [(G1_DOWN, g1_send, False), (G1_UP, g1_send, True)]
     events += [(G2_WHEN, g2_send), (G3_WHEN, g3_send), (ORDER_WHEN, g_order), (OWN_WHEN, fold, 0, CHUNKS)]
-    events += [(SECOND_WHEN, fold, 1, [c for c in CHUNKS if c[0] < min(FIRST)])]
+    events += [(SECOND_WHEN, fold, 1, [c for c in CHUNKS if c[0] < FIRST])]
     for _, what, *given in sorted(events, key=lambda e: e[0]):
         what(*given)
-    for dy in range(-3, 5):
-        rest(dy, False)
+    for b in (1, 2):
+        for p in range(NREST):
+            rest_wait(b, p)
 
     outs = []
     for k, (c0, n) in enumerate(CHUNKS):
         c = pl.ds(c0, n)
-        if c0 >= min(FIRST):
+        if c0 >= FIRST:
             fold(1, [(c0, n)])
         pair = [seq_grad(2, i, c) for i in (0, 1)]
         totals = [added(2, e, sums[e, :, c], pair) for e in range(EXAMPLES)]
@@ -284,6 +303,8 @@
     for b in (1, 2):
         for r in range(NR):
             z_out(r, b).wait_send()
+        for p in range(NREST):
+            rest(b, p).wait_send()
     for d in (1, 2, 3):
         g1_copy(d).wait_send()
     for c in sent:
@@ -310,6 +331,8 @@
             vmem((TOKENS // 2, OUT_TILE), jnp.bfloat16),
             vmem((TOKENS, OUT_TILE), jnp.bfloat16),
             vmem((EXAMPLES, OUT_TILE, IN_TILE), jnp.float32),
+            vmem((NY * BLK, IN_TILE - FIRST), jnp.bfloat16),
+            vmem((2, NY * BLK, IN_TILE - FIRST), jnp.bfloat16),
             vmem((OUT_TILE, IN_TILE), jnp.float32),
             dma((2,)),
             dma((len(CHUNKS),)),
@@ -317,8 +340,8 @@
             dma((2 * NR,)),
             dma((len(UNITS) * 8,)),
             dma((len(UNITS) * 8,)),
-            dma((16 * NR,)),
-            dma((16 * NR,)),
+            dma((2 * NREST,)),
+            dma((2 * NREST,)),
             dma((3,)),
             dma((3,)),
             dma((3,)),

time: 75.7 us -> 74.7 us (0.987)
  the two profiles are of different devices: /device:TPU:72 before, /device:TPU:136 now
where the time goes in v3:
time: 74.7 us; the launch traced here: 74.5 us
  Pallas kernels  72.4 us (97%)
  local copies, waits for them, and re-layouts  2.16 us (3%)
    pallas_call x1, Pallas kernels, on_device(): pl.pallas_call(body, out_shape=jax.ShapeDtypeStruct((OUT_TILE, IN_TILE),...  72.4 us
    unnamed x1, local copies, waits for them, and re-layouts  2.16 us

profile of v3, /device:TPU:136, one launch (start us, length us, event | category | flops | bytes accessed | tf_op | source)
XLA Modules:
  0.0 74.5 jit_solution(10711287871302375388)
XLA Ops:
  0.0 72.4 %gather_and_correct.1 = f32[256,896]{1,0:T(8,128)} custom-call(s32[6]{0:T(128)} %seq_ref.1, bf16[128,896]{1,0:T(8,128)(2,1)} %acts_ref.1, bf16[96,256]{1,0:T(8,128)(2,1)} %grads_ref.1), custom_call_target="tpu_custom_call" | custom-call | flops 1409286144 | bytes 917504 | tf_op jit(solution)/shard_map/gather_and_correct/pallas_call | solution.py:319
  72.4 2.2 %copy.5 = f32[256,896]{1,0:T(8,128)} copy(f32[256,896]{1,0:T(8,128)} %gather_and_correct.1) | data formatting | bytes 1835008
